TPU v7x, 256 devices: a whole 4x4x8 slice. The times are simulated.
256 devices in a mesh: tm: 64 (over x, z, core), space: 4 (over y).
Axes of the slice: x: 4, y: 4, z: 8, core: 2. Of those that a mesh axis runs over, the one named last changes fastest.
Arguments:
- misfit: bfloat16 [512, 32, 64, 128], P('tm', 'space'), may hold values from -2 to 2
- guess: float32 [64, 32, 64, 128], P('tm', 'space'), may hold values from -4 to 4
- rate: float32 [64, 32, 64, 128], P('tm', 'space'), may hold values from 5e-05 to 1.7
- coeffs: float32 [3, 32, 64, 128], P(None, 'space'), may hold values from -0.25 to 0.25
- control: float32 [32, 64, 128], P('space'), may hold values from -6 to 6
Outputs:
- corrected: float32 [64, 32, 64, 128], P('tm', 'space')
- gradient: float32 [32, 64, 128], P('space')
All inputs are finite; a program needn't handle non-finite values.
Results may differ from a plain program's by a relative error of at most 0.0003.
Values sent between devices are 32-bit elements; how exact they have to be, the bound alone decides.
A program may use at most 128 MiB of HBM per device.

v0:
```python
import jax
import jax.numpy as jnp
from jax import lax
from jax.sharding import PartitionSpec as P

STEPS = 8


NU = 0.14
BETA = 0.5


def passed_along(array, axis, by):
    devices = lax.axis_size(axis)
    pairs = [(i, i + by) for i in range(devices) if 0 <= i + by < devices]
    return lax.ppermute(array, axis, pairs)


def extended(block, sides, width):
    for axis, dim in sides:
        count = lax.axis_size(axis)
        forward = [(i, i + 1) for i in range(count - 1)]
        backward = [(target, source) for source, target in forward]
        low = lax.ppermute(
            lax.slice_in_dim(block, block.shape[dim] - width, None, axis=dim), axis, forward
        )
        high = lax.ppermute(lax.slice_in_dim(block, 0, width, axis=dim), axis, backward)
        block = jnp.concatenate([low, block, high], axis=dim)
    return block


def prefix(value, axis, join, neutral):
    count, mine = (lax.axis_size(axis), lax.axis_index(axis))
    pieces = jax.tree.map(lambda part: lax.all_gather(part, axis), value)
    pieces = jax.tree.map(lambda part: part[::-1], pieces)
    mine = count - 1 - mine
    total = jax.tree.map(
        lambda part, zero: jnp.full_like(part, 0) + jnp.asarray(zero, part.dtype), value, neutral
    )

    def turn(position, total):
        longer = join(total, jax.tree.map(lambda part: part[position], pieces))
        return jax.tree.map(lambda new, old: jnp.where(position < mine, new, old), longer, total)

    return lax.fori_loop(0, count - 1, turn, total)


def advance(wide_field, wide_coeffs, forcing):
    inner = wide_field[1:-1]
    inner_coeffs = wide_coeffs[:, 1:-1]
    padded = jnp.pad(inner, ((0, 0), (1, 1), (1, 1)))
    beside = wide_field[2:] + wide_field[:-2]
    beside = beside + padded[:, 2:, 1:-1] + padded[:, :-2, 1:-1]
    beside = beside + padded[:, 1:-1, 2:] + padded[:, 1:-1, :-2]
    flux_x = wide_coeffs[0] * wide_field
    flux_y = jnp.pad(inner_coeffs[1] * inner, ((0, 0), (1, 1), (0, 0)))
    flux_z = jnp.pad(inner_coeffs[2] * inner, ((0, 0), (0, 0), (1, 1)))
    flow = (
        flux_x[2:]
        - flux_x[:-2]
        + (flux_y[:, 2:] - flux_y[:, :-2])
        + (flux_z[:, :, 2:] - flux_z[:, :, :-2])
    )
    return inner + NU * (beside - 6.0 * inner) + 0.5 * flow + forcing


def compose(earlier, later):
    return (later[0] * earlier[0], later[0] * earlier[1] + later[1])


def on_device(misfit, guess, rate, coeffs, control):
    own_guess = guess[0]
    zeros_field = jnp.zeros_like(own_guess)
    next_guess = passed_along(own_guess, "tm", -1)
    coeff_rows = extended(coeffs, (("space", 1),), 1)

    def relax(start, count):
        field = start
        summed = zeros_field
        for turn in range(count):
            step_index = STEPS - 1 - turn
            current = extended(field, (("space", 0),), 1)
            field = advance(current, coeff_rows, misfit[step_index].astype(jnp.float32))
            summed = summed + field
        return (field, summed)

    arrived, unused_sum = relax(next_guess, STEPS)
    residual = arrived - own_guess
    factor = jnp.exp(-rate[0])
    carried = prefix((factor, residual), "tm", compose, (jnp.ones_like(factor), zeros_field))
    later_error = carried[1]
    corrected = own_guess + (factor * later_error + residual)
    next_corrected = passed_along(corrected, "tm", -1)
    unused_field, partial_value = relax(next_corrected, STEPS - 1)
    total = lax.psum(partial_value + corrected, "tm")
    gradient = BETA * control + total / (lax.axis_size("tm") * STEPS)
    return (corrected[None], gradient)


def solution(mesh):
    placed = (
        P("tm", "space", None, None),
        P("tm", "space", None, None),
        P("tm", "space", None, None),
        P(None, "space", None, None),
        P("space", None, None),
    )
    return jax.shard_map(
        on_device,
        mesh=mesh,
        in_specs=placed,
        out_specs=(P("tm", "space", None, None), P("space", None, None)),
        check_vma=False,
    )
```

profile of v0, /device:TPU:1, one launch (start us, length us, event | category | flops | bytes accessed | tf_op | source)
XLA Modules:
  0.0 556.2 jit_solution(7130430088844454983)
XLA Ops:
  9.1 5.2 collective-permute-start
  19.6 4.4 collective-permute-start.2
  28.8 4.1 collective-permute-start.6
  36.7 4.7 collective-permute-start.8
  43.8 3.6 collective-permute-start.10
  49.7 2.8 collective-permute-done.9
  54.2 4.4 collective-permute-start.12
  61.3 4.3 collective-permute-start.14
  68.3 4.3 collective-permute-start.16
  75.3 4.7 collective-permute-start.18
  82.2 33.1 %all-gather.4.cloned.1.call-done = f32[64,8,64,128]{3,2,1,0:T(8,128)} async-done(((f32[1,8,64,128]{3,2,1,0:T(8,128)}), f32[64,8,64,128]{3,2,1,0:T(8,128)}) %all-gather.4.cloned.1.call-update) | async-done | bytes 16777232 | tf_op jit(solution)/shard_map/all_gather | solution.py:34
  115.3 11.9 %rev.6 = f32[64,8,64,128]{3,2,1,0:T(8,128)} reverse(f32[64,8,64,128]{3,2,1,0:T(8,128)} %all-gather.4.cloned.1.call-done), dimensions={0} | reverse | bytes 33554432 | tf_op jit(solution)/shard_map/rev | solution.py:35
  127.2 88.2 %all-gather.6.cloned.1.call-done = f32[512,64,128]{2,1,0:T(8,128)} async-done(((f32[8,64,128]{2,1,0:T(8,128)}), f32[512,64,128]{2,1,0:T(8,128)}) %all-gather.6.cloned.1.call-update) | async-done | bytes 16777232 | tf_op jit(solution)/shard_map/all_gather | solution.py:34
  215.4 11.9 %rev.7 = f32[64,8,64,128]{3,2,1,0:T(8,128)} reverse(f32[64,8,64,128]{3,2,1,0:T(8,128)} %bitcast.102), dimensions={0} | reverse | bytes 33554432 | tf_op jit(solution)/shard_map/rev | solution.py:35
  227.3 80.5 %while.14 = (s32[]{:T(128)}, f32[8,64,128]{2,1,0:T(8,128)S(1)}, s32[]{:T(128)}, f32[64,8,64,128]{3,2,1,0:T(8,128)}, f32[64,8,64,128]{3,2,1,0:T(8,128)}, /*index=5*/s32[]{:T(128)}, s32[]{:T(128)}) while((s32[]{:T(128)}, f32[8,64,128]{2,1,0:T(8,128)S(1)}, s32[]{:T(128)}, f32[64,8,64,128]{3,2,1,0:T(8,128)}, ...), condition=%wide.region_1.2_spmd.clone, body=%wide.region_0.1_spmd.clone.sunk | while | flops 262148 | bytes 1048677 | solution.py:45
  310.0 5.5 collective-permute-done.19
  316.8 4.0 collective-permute-start.21
  323.6 4.3 collective-permute-start.23
  330.6 4.3 collective-permute-start.25
  337.6 4.3 collective-permute-start.27
  344.6 4.7 collective-permute-start.29
  352.1 4.3 collective-permute-start.31
  359.1 4.6 collective-permute-start.33
  365.9 181.9 %all-reduce.47.cloned.1.call-done = f32[8,64,128]{2,1,0:T(8,128)} async-done(((f32[8,64,128]{2,1,0:T(8,128)}), f32[8,64,128]{2,1,0:T(8,128)}) %all-reduce.47.cloned.1.call-update) | async-done | bytes 262160 | tf_op jit(solution)/shard_map/psum | solution.py:95
  (196 shorter events, 135.1 us)
Async XLA Ops:
  7.2 108.1 %all-gather.4.cloned.1.call-start = ((), (), s32[]{:S(2)}) async-start(), calls=%async_computation | async-start | bytes 17039360 | tf_op jit(solution)/shard_map/all_gather | solution.py:34
  9.1 206.3 %all-gather.6.cloned.1.call-start = ((), (), s32[]{:S(2)}) async-start(), calls=%async_computation.2 | async-start | bytes 17039360 | tf_op jit(solution)/shard_map/all_gather | solution.py:34
  9.1 9.2 %collective-permute-start = (f32[8,64,128]{2,1,0:T(8,128)}, f32[8,64,128]{2,1,0:T(8,128)S(1)}, u32[]{:S(2)}, u32[]{:S(2)}) collective-permute-start(f32[8,64,128]{2,1,0:T(8,128)} %bitcast.104), channel_id=1, source_target_pairs={{4,0},{8,4},{12,8},{16,12},{20,16},{24,20},{28,24},{32,28},{36,32}... | collective-permute-start | bytes 786440 | tf_op jit(solution)/shard_map/ppermute | solution.py:16
  15.2 9.8 %collective-permute-start.3 = (f32[3,1,64,128]{3,2,1,0:T(8,128)S(1)}, f32[3,1,64,128]{3,2,1,0:T(8,128)S(1)}, u32[]{:S(2)}, u32[]{:S(2)}) collective-permute-start(f32[3,1,64,128]{3,2,1,0:T(8,128)S(1)} %get-tuple-element.157), channel_id=1, source_target_pairs={{0,1},{1,2},{2,3},{4,5},{5,6},{6,7},{8,9},{9,10},{10,11},{12,13},{... | collective-permute-start | bytes 294920 | tf_op jit(solution)/shard_map/ppermute | solution.py:24
  16.7 8.4 %collective-permute-start.4 = (f32[3,1,64,128]{3,2,1,0:T(8,128)S(1)}, f32[3,1,64,128]{3,2,1,0:T(8,128)S(1)}, u32[]{:S(2)}, u32[]{:S(2)}) collective-permute-start(f32[3,1,64,128]{3,2,1,0:T(8,128)S(1)} %get-tuple-element.158), channel_id=1, source_target_pairs={{1,0},{2,1},{3,2},{5,4},{6,5},{7,6},{9,8},{10,9},{11,10},{13,12},{... | collective-permute-start | bytes 294920 | tf_op jit(solution)/shard_map/ppermute | solution.py:27
  18.3 6.8 %collective-permute-start.1 = (f32[1,64,128]{2,1,0:T(8,128)S(1)}, f32[1,64,128]{2,1,0:T(8,128)S(1)}, u32[]{:S(2)}, u32[]{:S(2)}) collective-permute-start(f32[1,64,128]{2,1,0:T(8,128)S(1)} %get-tuple-element.188), channel_id=1, source_target_pairs={{1,0},{2,1},{3,2},{5,4},{6,5},{7,6},{9,8},{10,9},{11,10},{13,12},{... | collective-permute-start | bytes 98312 | tf_op jit(solution)/shard_map/ppermute | solution.py:27
  27.5 6.4 %collective-permute-start.5 = (f32[1,64,128]{2,1,0:T(8,128)S(1)}, f32[1,64,128]{2,1,0:T(8,128)S(1)}, u32[]{:S(2)}, u32[]{:S(2)}) collective-permute-start(f32[1,64,128]{2,1,0:T(8,128)S(1)} %get-tuple-element.186), channel_id=1, source_target_pairs={{1,0},{2,1},{3,2},{5,4},{6,5},{7,6},{9,8},{10,9},{11,10},{13,12},{... | collective-permute-start | bytes 98312 | tf_op jit(solution)/shard_map/ppermute | solution.py:27
  35.4 7.0 %collective-permute-start.7 = (f32[1,64,128]{2,1,0:T(8,128)S(1)}, f32[1,64,128]{2,1,0:T(8,128)S(1)}, u32[]{:S(2)}, u32[]{:S(2)}) collective-permute-start(f32[1,64,128]{2,1,0:T(8,128)S(1)} %get-tuple-element.184), channel_id=1, source_target_pairs={{1,0},{2,1},{3,2},{5,4},{6,5},{7,6},{9,8},{10,9},{11,10},{13,12},{... | collective-permute-start | bytes 98312 | tf_op jit(solution)/shard_map/ppermute | solution.py:27
  36.7 5.7 %collective-permute-start.8 = (f32[1,64,128]{2,1,0:T(8,128)S(1)}, f32[1,64,128]{2,1,0:T(8,128)S(1)}, u32[]{:S(2)}, u32[]{:S(2)}) collective-permute-start(f32[1,64,128]{2,1,0:T(8,128)S(1)} %get-tuple-element.183), channel_id=1, source_target_pairs={{0,1},{1,2},{2,3},{4,5},{5,6},{6,7},{8,9},{9,10},{10,11},{12,13},{... | collective-permute-start | bytes 98312 | tf_op jit(solution)/shard_map/ppermute | solution.py:24
  43.8 5.9 %collective-permute-start.10 = (f32[1,64,128]{2,1,0:T(8,128)S(1)}, f32[1,64,128]{2,1,0:T(8,128)S(1)}, u32[]{:S(2)}, u32[]{:S(2)}) collective-permute-start(f32[1,64,128]{2,1,0:T(8,128)S(1)} %get-tuple-element.181), channel_id=1, source_target_pairs={{0,1},{1,2},{2,3},{4,5},{5,6},{6,7},{8,9},{9,10},{10,11},{12,13},{... | collective-permute-start | bytes 98312 | tf_op jit(solution)/shard_map/ppermute | solution.py:24
  52.9 5.7 %collective-permute-start.11 = (f32[1,64,128]{2,1,0:T(8,128)S(1)}, f32[1,64,128]{2,1,0:T(8,128)S(1)}, u32[]{:S(2)}, u32[]{:S(2)}) collective-permute-start(f32[1,64,128]{2,1,0:T(8,128)S(1)} %get-tuple-element.180), channel_id=1, source_target_pairs={{1,0},{2,1},{3,2},{5,4},{6,5},{7,6},{9,8},{10,9},{11,10},{13,12},{... | collective-permute-start | bytes 98312 | tf_op jit(solution)/shard_map/ppermute | solution.py:27
  60.0 5.6 %collective-permute-start.13 = (f32[1,64,128]{2,1,0:T(8,128)S(1)}, f32[1,64,128]{2,1,0:T(8,128)S(1)}, u32[]{:S(2)}, u32[]{:S(2)}) collective-permute-start(f32[1,64,128]{2,1,0:T(8,128)S(1)} %get-tuple-element.178), channel_id=1, source_target_pairs={{1,0},{2,1},{3,2},{5,4},{6,5},{7,6},{9,8},{10,9},{11,10},{13,12},{... | collective-permute-start | bytes 98312 | tf_op jit(solution)/shard_map/ppermute | solution.py:27
  67.0 5.6 %collective-permute-start.15 = (f32[1,64,128]{2,1,0:T(8,128)S(1)}, f32[1,64,128]{2,1,0:T(8,128)S(1)}, u32[]{:S(2)}, u32[]{:S(2)}) collective-permute-start(f32[1,64,128]{2,1,0:T(8,128)S(1)} %get-tuple-element.176), channel_id=1, source_target_pairs={{1,0},{2,1},{3,2},{5,4},{6,5},{7,6},{9,8},{10,9},{11,10},{13,12},{... | collective-permute-start | bytes 98312 | tf_op jit(solution)/shard_map/ppermute | solution.py:27
  74.0 6.0 %collective-permute-start.17 = (f32[1,64,128]{2,1,0:T(8,128)S(1)}, f32[1,64,128]{2,1,0:T(8,128)S(1)}, u32[]{:S(2)}, u32[]{:S(2)}) collective-permute-start(f32[1,64,128]{2,1,0:T(8,128)S(1)} %get-tuple-element.174), channel_id=1, source_target_pairs={{1,0},{2,1},{3,2},{5,4},{6,5},{7,6},{9,8},{10,9},{11,10},{13,12},{... | collective-permute-start | bytes 98312 | tf_op jit(solution)/shard_map/ppermute | solution.py:27
  75.3 5.7 %collective-permute-start.18 = (f32[1,64,128]{2,1,0:T(8,128)S(1)}, f32[1,64,128]{2,1,0:T(8,128)S(1)}, u32[]{:S(2)}, u32[]{:S(2)}) collective-permute-start(f32[1,64,128]{2,1,0:T(8,128)S(1)} %get-tuple-element.173), channel_id=1, source_target_pairs={{0,1},{1,2},{2,3},{4,5},{5,6},{6,7},{8,9},{9,10},{10,11},{12,13},{... | collective-permute-start | bytes 98312 | tf_op jit(solution)/shard_map/ppermute | solution.py:24
  82.2 465.7 %all-reduce.47.cloned.1.call-start = ((), (), s32[]{:S(2)}) async-start(), calls=%async_computation.1 | async-start | bytes 524288 | tf_op jit(solution)/shard_map/psum | solution.py:95
  307.9 7.7 %collective-permute-start.19 = (f32[8,64,128]{2,1,0:T(8,128)S(1)}, f32[8,64,128]{2,1,0:T(8,128)S(1)}, u32[]{:S(2)}, u32[]{:S(2)}) collective-permute-start(f32[8,64,128]{2,1,0:T(8,128)S(1)} %fusion.217), channel_id=1, source_target_pairs={{4,0},{8,4},{12,8},{16,12},{20,16},{24,20},{28,24},{32,28},{36,32}... | collective-permute-start | bytes 786440 | tf_op jit(solution)/shard_map/ppermute | solution.py:16
  322.3 5.6 %collective-permute-start.22 = (f32[1,64,128]{2,1,0:T(8,128)S(1)}, f32[1,64,128]{2,1,0:T(8,128)S(1)}, u32[]{:S(2)}, u32[]{:S(2)}) collective-permute-start(f32[1,64,128]{2,1,0:T(8,128)S(1)} %get-tuple-element.170), channel_id=1, source_target_pairs={{1,0},{2,1},{3,2},{5,4},{6,5},{7,6},{9,8},{10,9},{11,10},{13,12},{... | collective-permute-start | bytes 98312 | tf_op jit(solution)/shard_map/ppermute | solution.py:27
  329.3 5.6 %collective-permute-start.24 = (f32[1,64,128]{2,1,0:T(8,128)S(1)}, f32[1,64,128]{2,1,0:T(8,128)S(1)}, u32[]{:S(2)}, u32[]{:S(2)}) collective-permute-start(f32[1,64,128]{2,1,0:T(8,128)S(1)} %get-tuple-element.168), channel_id=1, source_target_pairs={{1,0},{2,1},{3,2},{5,4},{6,5},{7,6},{9,8},{10,9},{11,10},{13,12},{... | collective-permute-start | bytes 98312 | tf_op jit(solution)/shard_map/ppermute | solution.py:27
  336.3 5.6 %collective-permute-start.26 = (f32[1,64,128]{2,1,0:T(8,128)S(1)}, f32[1,64,128]{2,1,0:T(8,128)S(1)}, u32[]{:S(2)}, u32[]{:S(2)}) collective-permute-start(f32[1,64,128]{2,1,0:T(8,128)S(1)} %get-tuple-element.166), channel_id=1, source_target_pairs={{1,0},{2,1},{3,2},{5,4},{6,5},{7,6},{9,8},{10,9},{11,10},{13,12},{... | collective-permute-start | bytes 98312 | tf_op jit(solution)/shard_map/ppermute | solution.py:27
  343.3 6.1 %collective-permute-start.28 = (f32[1,64,128]{2,1,0:T(8,128)S(1)}, f32[1,64,128]{2,1,0:T(8,128)S(1)}, u32[]{:S(2)}, u32[]{:S(2)}) collective-permute-start(f32[1,64,128]{2,1,0:T(8,128)S(1)} %get-tuple-element.164), channel_id=1, source_target_pairs={{1,0},{2,1},{3,2},{5,4},{6,5},{7,6},{9,8},{10,9},{11,10},{13,12},{... | collective-permute-start | bytes 98312 | tf_op jit(solution)/shard_map/ppermute | solution.py:27
  344.6 5.8 %collective-permute-start.29 = (f32[1,64,128]{2,1,0:T(8,128)S(1)}, f32[1,64,128]{2,1,0:T(8,128)S(1)}, u32[]{:S(2)}, u32[]{:S(2)}) collective-permute-start(f32[1,64,128]{2,1,0:T(8,128)S(1)} %get-tuple-element.163), channel_id=1, source_target_pairs={{0,1},{1,2},{2,3},{4,5},{5,6},{6,7},{8,9},{9,10},{10,11},{12,13},{... | collective-permute-start | bytes 98312 | tf_op jit(solution)/shard_map/ppermute | solution.py:24
  350.8 5.6 %collective-permute-start.30 = (f32[1,64,128]{2,1,0:T(8,128)S(1)}, f32[1,64,128]{2,1,0:T(8,128)S(1)}, u32[]{:S(2)}, u32[]{:S(2)}) collective-permute-start(f32[1,64,128]{2,1,0:T(8,128)S(1)} %get-tuple-element.162), channel_id=1, source_target_pairs={{1,0},{2,1},{3,2},{5,4},{6,5},{7,6},{9,8},{10,9},{11,10},{13,12},{... | collective-permute-start | bytes 98312 | tf_op jit(solution)/shard_map/ppermute | solution.py:27
  357.8 5.9 %collective-permute-start.32 = (f32[1,64,128]{2,1,0:T(8,128)S(1)}, f32[1,64,128]{2,1,0:T(8,128)S(1)}, u32[]{:S(2)}, u32[]{:S(2)}) collective-permute-start(f32[1,64,128]{2,1,0:T(8,128)S(1)} %get-tuple-element.160), channel_id=1, source_target_pairs={{1,0},{2,1},{3,2},{5,4},{6,5},{7,6},{9,8},{10,9},{11,10},{13,12},{... | collective-permute-start | bytes 98312 | tf_op jit(solution)/shard_map/ppermute | solution.py:27
  (19 other events, 658.1 us)
Sparse Core Ops, SparseCore 0:
  11.4 103.8 all-gather.3
  118.6 96.6 all-gather.5
  366.0 181.7 all-reduce.46
where the time goes:
time: 559 us; the launch traced here: 556 us
  waiting for transfers between devices  322 us (58%)
  other arithmetic  98.8 us (18%)
  starting transfers between devices  94.4 us (17%)
  local copies, waits for them, and re-layouts  24.9 us (4%)
  between operations  14.5 us (3%)
    psum x1, waiting for transfers between devices, on_device(): total = lax.psum(partial_value + corrected, 'tm')  182 us
    all_gather x2, waiting for transfers between devices, prefix(): pieces = jax.tree.map(lambda part: lax.all_gather(part, axis), value)  121 us
    select_n x63, other arithmetic, turn(): jnp.where(position < mine, new, old)  79.1 us
    ppermute x16, starting transfers between devices, extended(): lax.ppermute(lax.slice_in_dim(block, block.shape[dim] - width, None, axis...  66.3 us
    rev x2, local copies, waits for them, and re-layouts, prefix(): pieces = jax.tree.map(lambda part: part[::-1], pieces)  23.8 us
    ppermute x16, starting transfers between devices, extended(): lax.ppermute(lax.slice_in_dim(block, 0, width, axis=dim), axis, backward)  20.7 us
  transfers between devices with their start and end apart: 37, of which 17 were waited for; matrix products, arithmetic and copies ran while one was open for 5% of the time, Pallas kernels for 0%

commit v1 on v0

v1 whole, which is shorter than its diff:
```python
import functools
from types import SimpleNamespace

import jax
import jax.numpy as jnp
from jax import lax
from jax.experimental import pallas as pl
from jax.experimental.pallas import tpu as pltpu
from jax.sharding import PartitionSpec as P

NU = 0.14
BETA = 0.5
CENTRE = 1.0 - 6.0 * NU
ROUNDS = (1, 1, 2, 2, 2)
CUT = 99
MESH = pl.DeviceIdType.MESH
F32 = jnp.float32
MAX_MOVES = 64
LOW, HIGH = 0, 1
TIME, SPACE = "tm", "space"


def rolled(value, by, axis):
    return pltpu.roll(value, by % value.shape[axis], axis)


def when(condition, run):
    def body():
        run()

    if condition is None:
        body()
    else:
        pl.when(condition)(body)


class Net:
    def __init__(self, send, recv, here):
        self.send, self.recv, self.here, self.moves = send, recv, here, []

    def move(self, whole, sent=None, got=None):
        return Move(self, whole, sent, got)

    def close(self):
        for move in self.moves:
            move.close()


class Move:
    def __init__(self, net, whole, sent, got):
        self.net, self.whole, self.sent, self.got = net, whole, sent, got
        self.index, self.started, self.arrived = len(net.moves), False, False
        net.moves.append(self)

    def copy(self, src, dst, device):
        return pltpu.make_async_remote_copy(
            src_ref=src, dst_ref=dst, send_sem=self.net.send.at[self.index], recv_sem=self.net.recv.at[self.index],
            device_id=device, device_id_type=MESH,
        )

    def start(self, src, dst, device):
        self.started = True
        when(self.sent, lambda: self.copy(src, dst, device).start())
        return self

    def land(self):
        self.arrived = True
        when(self.got, lambda: self.copy(self.whole, self.whole, self.net.here).wait_recv())

    def close(self):
        if self.started:
            if not self.arrived:
                self.land()
            when(self.sent, lambda: self.copy(self.whole, self.whole, self.net.here).wait_send())


def kernel(cfg, misfit_in, guess_in, rate_in, coeffs_in, e_out, total_out, *scratch):
    buf = SimpleNamespace(**dict(zip(cfg.names, scratch)))
    wf = scratch[len(cfg.names):len(cfg.names) + len(cfg.rounds)]
    mids = scratch[len(cfg.names) + len(cfg.rounds):-4]
    misfit, inputs = scratch[-4], scratch[-3]
    guess, rate, coeffs = buf.guess, buf.rate, buf.coeffs
    fetches = [
        pltpu.make_async_copy(src, dst, inputs.at[i])
        for i, (src, dst) in enumerate(((guess_in, guess), (coeffs_in, coeffs), (misfit_in, misfit), (rate_in, rate)))
    ]
    for fetch in fetches:
        fetch.start()
    steps, rounds, rows, mid, lanes = cfg.steps, cfg.rounds, cfg.rows, cfg.mid, cfg.lanes
    groups, ny = cfg.groups, cfg.ny
    half, members, wide = mid // 2, 2 * rows, steps - 1
    deepest = max(rounds)
    slabs = groups * members

    tm, y = lax.axis_index(TIME), lax.axis_index(SPACE)
    x, spot = tm // members, tm % members
    z, core = spot // 2, spot % 2
    base = x * members
    has_low, has_high = y > 0, y < ny - 1
    has_next, has_before = tm < slabs - 1, tm > 0
    below, above, sibling = (tm, y - 1), (tm, y + 1), (base + spot + 1 - 2 * core, y)

    net = Net(scratch[-2], scratch[-1], (tm, y))
    ax, bx, ay, by, az, bz = buf.ax, buf.bx, buf.ay, buf.by, buf.az, buf.bz
    mine = pl.ds(pl.multiple_of(core * half, half), half)
    other = pl.ds(pl.multiple_of((1 - core) * half, half), half)
    rows_own, rows_low, rows_high = pl.ds(wide, rows), pl.ds(0, wide), pl.ds(wide + rows, wide)

    barrier = pltpu.get_barrier_semaphore()

    def greet(device):
        pl.semaphore_signal(barrier, inc=1, device_id=device, device_id_type=MESH)

    def greet_member(i, _):
        greet((base + (spot + i) % members, y))
        return 0

    lax.fori_loop(1, members, greet_member, 0)
    for i in range(1, groups):
        greet(((x + i) % groups * members + spot, y))
    when(has_low, lambda: greet(below))
    when(has_high, lambda: greet(above))
    for exists, there in ((has_next, tm + 1), (has_before, tm - 1)):
        when(exists, lambda: greet((there, y)))
        when(exists & has_low, lambda: greet((there, y - 1)))
        when(exists & has_high, lambda: greet((there, y + 1)))
    sides = has_low.astype(jnp.int32) + has_high.astype(jnp.int32)
    ends = has_next.astype(jnp.int32) + has_before.astype(jnp.int32)

    for fetch in fetches:
        fetch.wait()
    for r, n in enumerate(rounds):
        for s in range(n - 1):
            k, turn, width = cfg.forcing_at[(r, s)], sum(rounds[:r]) + s, n - 1 - s
            for i in range(width):
                buf.f_send[LOW, k + i] = misfit[steps - 1 - turn, rows - width + i].astype(F32)
                buf.f_send[HIGH, k + i] = misfit[steps - 1 - turn, i].astype(F32)

    pl.semaphore_wait(barrier, members - 1 + groups - 1 + sides + ends + sides * ends)
    if cfg.cut == 0:
        return net.close()

    first = rounds[0]
    start = net.move(wf[0].at[pl.ds(first, rows)], has_before, has_next)
    start.start(guess, wf[0].at[pl.ds(first, rows)], (tm - 1, y))

    def up_down(low, high, whole_low, whole_high):
        up = net.move(whole_low, has_high, has_low)
        down = net.move(whole_high, has_low, has_high)
        up.start(low[0], low[1], above)
        down.start(high[0], high[1], below)
        return up, down

    lows, highs = wf[0].at[pl.ds(0, first)], wf[0].at[pl.ds(first + rows, first)]
    start_up = net.move(lows, has_before & has_high, has_next & has_low)
    start_up.start(guess.at[pl.ds(rows - first, first)], lows, (tm - 1, y + 1))
    start_down = net.move(highs, has_before & has_low, has_next & has_high)
    start_down.start(guess.at[pl.ds(0, first)], highs, (tm - 1, y - 1))
    start_faces = (start_up, start_down)

    def both_ends(src, at_low, at_high, dst):
        return up_down((src.at[at_high], dst.at[LOW]), (src.at[at_low], dst.at[HIGH]), dst.at[LOW], dst.at[HIGH])

    def ends(src, width, dst, at=0):
        low, high = pl.ds(at, width), pl.ds(rows - at - width, width)
        to_low, to_high = pl.ds(deepest - at - width, width), pl.ds(at, width)
        up, down = dst.at[LOW, to_low], dst.at[HIGH, to_high]
        return up_down((src.at[high], up), (src.at[low], down), up, down)

    beside = ends(coeffs.at[0], 1, buf.cx)
    further = []
    if deepest > 1:
        count = deepest - 1
        further.append(ends(coeffs.at[0], count, buf.cx, 1))
        for i in range(2):
            low, high = buf.cyz.at[LOW, i], buf.cyz.at[HIGH, i]
            further.append(up_down(
                (coeffs.at[1 + i, pl.ds(rows - count, count)], low), (coeffs.at[1 + i, pl.ds(0, count)], high), low, high))
        low, high = buf.f_halo.at[LOW], buf.f_halo.at[HIGH]
        further.append(up_down((buf.f_send.at[LOW], low), (buf.f_send.at[HIGH], high), low, high))

    def transpose(src, dst):
        move = net.move(dst.at[pl.ds(0, members - 1)])

        def send(i, _):
            to = (spot + i) % members
            part = src.at[to // 2, pl.ds(pl.multiple_of(to % 2 * half, half), half)]
            move.start(part, dst.at[spot], (base + to, y))
            return 0

        lax.fori_loop(1, members, send, 0)
        dst[spot] = src[z, mine]
        return move

    def across(src, dst):
        move = net.move(dst.at[pl.ds(0, groups - 1)])
        for i in range(1, groups):
            move.start(src, dst.at[x], ((x + i) % groups * members + spot, y))
        dst[x] = src[...]
        return move

    def along(source, target, whole):
        move = net.move(whole)

        def send(i, _):
            to = (z + i) % rows
            move.start(source(to), target, (base + 2 * to + core, y))
            return 0

        lax.fori_loop(1, rows, send, 0)
        return move

    def factors_x(row, c):
        ax[row] = NU + 0.5 * c
        bx[row] = NU - 0.5 * c

    def factors_yz(row, cy, cz):
        place = lax.broadcasted_iota(jnp.int32, (mid, lanes), 0)
        ay[row] = jnp.where(place == 0, 0.0, NU + 0.5 * cy)
        by[row] = jnp.where(place == mid - 1, 0.0, NU - 0.5 * cy)
        place = lax.broadcasted_iota(jnp.int32, (mid, lanes), 1)
        az[row] = jnp.where(place == 0, 0.0, NU + 0.5 * cz)
        bz[row] = jnp.where(place == lanes - 1, 0.0, NU - 0.5 * cz)

    def each(start, stop, run, unroll=1):
        def one(i, _):
            run(i)
            return 0

        if stop > start:
            lax.fori_loop(start, stop, one, 0, unroll=unroll if (stop - start) % unroll == 0 else 1)

    def own_factors(i):
        factors_x(wide + i, coeffs[0, i])
        factors_yz(wide + i, coeffs[1, i], coeffs[2, i])

    each(0, rows, own_factors, 2)

    def clear(ref, start, count):
        def one(i):
            ref[i] = jnp.zeros((mid, lanes), F32)

        each(start, start + count, one)

    halos = [(ref, n) for ref, n in zip(wf[1:], rounds[1:])] + [(ref, deepest - 1) for ref in mids]
    halos += [(buf.e, wide), (buf.e1, wide), (buf.e2, wide)]

    @pl.when(jnp.logical_not(has_low))
    def _():
        clear(bx, 0, wide)
        for ref, n in halos:
            clear(ref, 0, n)

    @pl.when(jnp.logical_not(has_high))
    def _():
        clear(ax, wide + rows, wide)
        for ref, n in halos:
            clear(ref, n + rows, n)

    when(jnp.logical_not(has_next & has_low), lambda: clear(wf[0], 0, first))
    when(jnp.logical_not(has_next & has_high), lambda: clear(wf[0], first + rows, first))
    when(jnp.logical_not(has_next), lambda: clear(wf[0], first, rows))

    def stepped(src, at, row):
        w = src[at]
        place = row + wide
        value = CENTRE * w
        value = value + (ax[place + 1] * src[at + 1] + bx[place - 1] * src[at - 1])
        value = value + (rolled(ay[place] * w, -1, 0) + rolled(by[place] * w, 1, 0))
        return value + (rolled(az[place] * w, -1, 1) + rolled(bz[place] * w, 1, 1))

    def relax_row(r, s, row, side=None):
        n = rounds[r]
        turn = sum(rounds[:r]) + s
        src, shift = (wf[r], n) if s == 0 else (mids[s - 1], deepest - 1)
        if side is None:
            forcing = misfit[steps - 1 - turn, row].astype(F32)
        elif side == LOW:
            forcing = buf.f_halo[LOW, cfg.forcing_at[(r, s)] + (n - 1 - s) + row]
        else:
            forcing = buf.f_halo[HIGH, cfg.forcing_at[(r, s)] + row - rows]
        value = stepped(src, row + shift, row) + forcing
        if s < n - 1:
            mids[s][row + deepest - 1] = value
        elif r < len(rounds) - 1:
            wf[r + 1][row + rounds[r + 1]] = value
        if side is None:
            if turn == 0:
                buf.d[row] = guess[row] + value
            elif turn < steps - 1:
                buf.d[row] = buf.d[row] + value
            else:
                buf.res[row] = value - guess[row]

    def inner(r):
        for s in range(rounds[r]):
            each(s + 1, rows - 1 - s, lambda row: relax_row(r, s, row), 2)

    def outer(r, side):
        for s in range(rounds[r]):
            reach = rounds[r] - 1 - s
            if side == LOW:
                when(has_low, lambda: [relax_row(r, s, row, LOW) for row in range(-reach, 0)])
                for row in range(s + 1):
                    relax_row(r, s, row)
            else:
                when(has_high, lambda: [relax_row(r, s, row, HIGH) for row in range(rows, rows + reach)])
                for row in range(rows - 1 - s, rows):
                    relax_row(r, s, row)

    def beside_factors(side):
        if side == HIGH:
            factors_x(wide + rows, buf.cx[side, 0])
        else:
            factors_x(wide - 1, buf.cx[side, deepest - 1])

    def further_factors(side):
        at = wide + rows if side == HIGH else wide - deepest
        each(0, deepest, lambda i: factors_x(at + i, buf.cx[side, i]))
        at = wide + rows if side == HIGH else wide - deepest + 1
        each(0, deepest - 1, lambda i: factors_yz(at + i, buf.cyz[side, 0, i], buf.cyz[side, 1, i]))

    def decays():
        rates.land()
        last = members - 1
        factor = jnp.exp(-buf.rates[last])
        buf.decay[last] = factor
        buf.upto[last] = factor

        def one(i, carry):
            upto, summed = carry
            k = last - i
            factor = jnp.exp(-buf.rates[k])
            upto = factor * upto
            buf.decay[k] = factor
            buf.upto[k] = upto
            return upto, summed + jnp.where((k > 0) | (x > 0), upto, 0.0)

        buf.fx_send[0], buf.fx_send[1] = lax.fori_loop(1, members, one, (factor, factor))
        return across(buf.fx_send, buf.fx)

    start.land()
    if cfg.cut == 20:
        return net.close()
    faces = start_faces
    for r in range(len(rounds)):
        inner(r)
        if r == len(rounds) - 2:
            group_decay = decays()
        if r < len(rounds) - 1:
            n, ref = rounds[r + 1], wf[r + 1]
            low, high = ref.at[pl.ds(0, n)], ref.at[pl.ds(n + rows, n)]
            coming = net.move(low, has_high, has_low), net.move(high, has_low, has_high)
        for side, exists in ((LOW, has_low), (HIGH, has_high)):
            if r == 0:
                beside[side].land()
                when(exists, lambda: beside_factors(side))
            if rounds[r] > 1 and max((1,) + rounds[:r]) == 1:
                for pair in further:
                    pair[side].land()
                when(exists, lambda: further_factors(side))
            faces[side].land()
            outer(r, side)
            if r < len(rounds) - 1:
                if side == LOW:
                    coming[HIGH].start(ref.at[pl.ds(n, n)], high, below)
                else:
                    coming[LOW].start(ref.at[pl.ds(rows, n)], low, above)
        if cfg.cut == 1 + r:
            return net.close()
        if r == 0:
            rates = transpose(rate, buf.rates)
        if r < len(rounds) - 1:
            faces = coming

    terms = transpose(buf.res, buf.terms)
    pair = net.move(buf.d_pair).start(buf.d.at[:, other], buf.d_pair, sibling)
    far = up_down(
        (coeffs.at[:, pl.ds(rows - wide, wide), mine], buf.far.at[LOW, :, :, mine]),
        (coeffs.at[:, pl.ds(0, wide), mine], buf.far.at[HIGH, :, :, mine]),
        buf.far.at[LOW, :, :, mine], buf.far.at[HIGH, :, :, mine],
    )

    terms.land()
    if cfg.cut == 10:
        return net.close()
    last = members - 1
    value = buf.terms[last]
    buf.local[last] = value

    def solve(i, carry):
        value, summed = carry
        k = last - i
        value = buf.decay[k] * value + buf.terms[k]
        buf.local[k] = value
        return value, summed + jnp.where((k > 0) | (x > 0), value, 0.0)

    buf.rx_send[0], buf.rx_send[1] = lax.fori_loop(1, members, solve, (value, value))
    group_result = across(buf.rx_send, buf.rx)

    pair.land()

    def pair_sum(i):
        buf.d_chip[i] = buf.d[i, mine] + buf.d_pair[i]

    each(0, rows, pair_sum)
    ring = along(lambda to: buf.d_chip.at[to], buf.d_ring.at[z], buf.d_ring.at[pl.ds(0, rows - 1)])
    buf.d_ring[z] = buf.d_chip[z]

    far_pair = []
    for side, exists in ((LOW, has_low), (HIGH, has_high)):
        far[side].land()
        part = buf.far.at[side, :, :, mine]
        far_pair.append(net.move(part, exists, exists).start(part, part, sibling))

    group_decay.land()
    group_result.land()
    if cfg.cut == 11:
        return net.close()
    carry = jnp.zeros((half, lanes), F32)
    e_sum = carry
    for group in reversed(range(groups)):
        buf.carry[group] = carry
        e_sum = e_sum + (buf.rx[group, 1] + buf.fx[group, 1] * carry)
        carry = buf.rx[group, 0] + buf.fx[group, 0] * carry
    e, t = buf.e, buf.t
    e[wide + z, mine] = e_sum
    e_mine = e.at[wide + z, mine]
    e_ring = along(lambda to: e_mine, e_mine, e.at[pl.ds(wide, rows - 1), mine])
    buf.t_own[...] = e_sum + carry

    carry = buf.carry[x]

    def finish(k):
        buf.back[k] = buf.local[k] + buf.upto[k] * carry

    each(0, members, finish)
    back = net.move(buf.back.at[pl.ds(0, members - 1)])

    def send_back(i):
        to = (spot + i) % members
        back.start(buf.back.at[to], buf.e_own.at[z, mine], (base + to, y))

    each(1, members, send_back)
    buf.e_own[z, mine] = buf.back[spot]

    e_ring.land()
    if cfg.cut == 12:
        return net.close()
    e_faces = up_down(
        (e.at[pl.ds(rows, wide), mine], e.at[rows_low, mine]), (e.at[pl.ds(wide, wide), mine], e.at[rows_high, mine]),
        e.at[rows_low, mine], e.at[rows_high, mine],
    )
    e_pair = net.move(e.at[rows_own, mine]).start(e.at[rows_own, mine], e.at[rows_own, mine], sibling)

    ring.land()
    buf.dx_send[...] = lax.fori_loop(1, rows, lambda i, s: s + buf.d_ring[i], buf.d_ring[0])
    d_across = across(buf.dx_send, buf.dx)

    def far_factors(side):
        def one(i):
            row = wide + rows + i if side == HIGH else i
            factors_x(row, buf.far[side, 0, i])
            factors_yz(row, buf.far[side, 1, i], buf.far[side, 2, i])

        each(0, wide, one)

    for side, exists in ((LOW, has_low), (HIGH, has_high)):
        far_pair[side].land()
        when(exists, lambda: far_factors(side))

    e_pairs = [e_pair]
    for side, exists, where in ((LOW, has_low, rows_low), (HIGH, has_high, rows_high)):
        e_faces[side].land()
        part = e.at[where, mine]
        e_pairs.append(net.move(part, exists, exists).start(part, part, sibling))

    d_across.land()
    t_mine = buf.t_own[...]
    for group in range(groups):
        t_mine = t_mine + buf.dx[group]
    t[z, mine] = t_mine
    t_ring = along(lambda to: t.at[z, mine], t.at[z, mine], t.at[pl.ds(0, rows - 1), mine])

    for pair in e_pairs:
        pair.land()
    if cfg.cut == 13:
        return net.close()

    for s in range(steps - 1):
        if s == min(2, steps - 2):
            t_ring.land()
            t_pair = net.move(t.at[:, mine]).start(t.at[:, mine], t.at[:, mine], sibling)
        src = (e, buf.e1, buf.e2)[0 if s == 0 else 1 + (s - 1) % 2]
        dst = (buf.e1, buf.e2)[s % 2]
        reach = steps - 2 - s

        def halo_row(row):
            dst[row + wide] = stepped(src, row + wide, row)

        def own_row(row):
            value = stepped(src, row + wide, row)
            dst[row + wide] = value
            buf.sum[row] = value if s == 0 else buf.sum[row] + value

        when(has_low, lambda: each(-reach, 0, halo_row, 2))
        when(has_high, lambda: each(rows, rows + reach, halo_row, 2))
        each(0, rows, own_row, 2)

    back.land()
    e_out[...] = buf.e_own[...]
    t_pair.land()
    total_out[...] = t[...] + buf.sum[...]
    net.close()


def exchange(mesh, misfit, guess, rate, coeffs, rounds, cut):
    steps, rows, mid, lanes = misfit.shape
    members, half, wide = 2 * rows, mid // 2, steps - 1
    ny = mesh.shape[SPACE]
    groups = mesh.shape[TIME] // members
    deepest = max(rounds)
    forcing_at, count = {}, 0
    for r, n in enumerate(rounds):
        for s in range(n - 1):
            forcing_at[(r, s)] = count
            count += n - 1 - s
    plane, part = (mid, lanes), (half, lanes)
    field, long, slots = (rows,) + plane, (rows + 2 * wide,) + plane, (members,) + part
    shapes = dict(
        guess=field, rate=field, coeffs=(3,) + field,
        cx=(2, deepest) + plane, cyz=(2, 2, max(deepest - 1, 1)) + plane,
        f_send=(2, max(count, 1)) + plane, f_halo=(2, max(count, 1)) + plane,
        rates=slots, decay=slots, upto=slots, fx_send=(2,) + part, fx=(groups, 2) + part,
        res=field, d=field, d_pair=(rows,) + part, d_chip=(rows,) + part, d_ring=(rows,) + part,
        dx_send=part, dx=(groups,) + part, t_own=part,
        terms=slots, local=slots, rx_send=(2,) + part, rx=(groups, 2) + part,
        carry=(groups,) + part, back=slots, e_own=field, t=field, sum=field, far=(2, 3, wide) + plane,
        ax=long, bx=long, ay=long, by=long, az=long, bz=long, e=long, e1=long, e2=long,
    )
    extra = [(rows + 2 * n,) + plane for n in rounds] + [(rows + 2 * (deepest - 1),) + plane] * (deepest - 1)
    cfg = SimpleNamespace(
        names=list(shapes), steps=steps, rounds=rounds, rows=rows, mid=mid, lanes=lanes, groups=groups, ny=ny,
        forcing_at=forcing_at, cut=cut,
    )
    in_vmem, in_hbm = pl.BlockSpec(memory_space=pltpu.VMEM), pl.BlockSpec(memory_space=pltpu.HBM)
    return pl.pallas_call(
        functools.partial(kernel, cfg),
        out_shape=[jax.ShapeDtypeStruct(field, F32)] * 2,
        in_specs=[in_hbm] * 4,
        out_specs=[in_vmem] * 2,
        scratch_shapes=[pltpu.VMEM(shape, F32) for shape in list(shapes.values()) + extra]
        + [pltpu.VMEM(misfit.shape, misfit.dtype), pltpu.SemaphoreType.DMA((4,))]
        + [pltpu.SemaphoreType.DMA((MAX_MOVES,))] * 2,
        compiler_params=pltpu.CompilerParams(
            collective_id=0, has_side_effects=True, vmem_limit_bytes=60 * 1024 * 1024),
        name="cycle",
    )(misfit, guess, rate, coeffs)


def on_device(mesh, rounds, cut, misfit, guess, rate, coeffs, control):
    correction, total = exchange(mesh, misfit, guess[0], rate[0], coeffs, rounds, cut)
    corrected = guess[0] + correction
    gradient = BETA * control + total / (mesh.shape[TIME] * misfit.shape[0])
    return corrected[None], gradient


def solution(mesh, rounds=ROUNDS, cut=CUT):
    slab, block = P(TIME, SPACE, None, None), P(SPACE, None, None)
    return jax.shard_map(
        functools.partial(on_device, mesh, rounds, cut),
        mesh=mesh,
        in_specs=(slab, slab, slab, P(None, SPACE, None, None), block),
        out_specs=(slab, block),
        check_vma=False,
    )
```

time: 559 us -> 65.4 us (0.12)
  waiting for transfers between devices: 322 us -> 0 us
  other arithmetic: 98.8 us -> 2.47 us
  starting transfers between devices: 94.4 us -> 0 us
  Pallas kernels: 0 us -> 61.1 us
  local copies, waits for them, and re-layouts: 24.9 us -> 0.01 us
  between operations: 14.5 us -> 0.67 us
    psum x1 -> x0, waiting for transfers between devices: 182 us -> none  [on_device(): total = lax.psum(partial_value + corrected, 'tm')]
    all_gather x2 -> x0, waiting for transfers between devices: 121 us -> none  [prefix(): pieces = jax.tree.map(lambda part: lax.all_gather(part, axis), value)]
    ppermute x34 -> x0, starting transfers between devices: 94.2 us -> none  [the longest x16 66.3 us: extended(): lax.ppermute(lax.slice_in_dim(block, block.shape[dim] - width, None, axis...]
    select_n x63 -> x0, other arithmetic: 79.1 us -> none  [turn(): jnp.where(position < mine, new, old)]
    pallas_call x0 -> x1, Pallas kernels: none -> 61.1 us  [exchange(): pl.pallas_call(functools.partial(kernel, cfg), out_shape=[jax.ShapeDtypeS...]
    rev x2 -> x0, local copies, waits for them, and re-layouts: 23.8 us -> none  [prefix(): pieces = jax.tree.map(lambda part: part[::-1], pieces)]
    ppermute x34 -> x0, waiting for transfers between devices: 19.1 us -> none  [the longest x16 10.5 us: extended(): lax.ppermute(lax.slice_in_dim(block, block.shape[dim] - width, None, axis...]
    mul x43 -> x0, other arithmetic: 13.8 us -> none  [the longest x13 7.64 us: advance(): flux_z = jnp.pad(inner_coeffs[2] * inner, ((0, 0), (0, 0), (1, 1)))]
  transfers between devices with their start and end apart: 37 -> 0, of which waited for: 17 -> 0; matrix products, arithmetic and copies ran while one was open for 5% -> 0% of each run, Pallas kernels for 0% -> 0%
where the time goes in v1:
time: 65.4 us; the launch traced here: 64.3 us
  Pallas kernels  61.1 us (93%)
  other arithmetic  2.47 us (4%)
  between operations  0.67 us (1%)
    pallas_call x1, Pallas kernels, exchange(): pl.pallas_call(functools.partial(kernel, cfg), out_shape=[jax.ShapeDtypeS...  61.1 us
    broadcast_in_dim x1, other arithmetic, on_device(): return (corrected[None], gradient)  1.74 us

profile of v1, /device:TPU:1, one launch (start us, length us, event | category | flops | bytes accessed | tf_op | source)
XLA Modules:
  0.0 64.3 jit_solution(8015885241507492440)
XLA Ops:
  0.6 0.0 copy-start
  0.6 61.1 %cycle.1 = (f32[8,64,128]{2,1,0:T(8,128)}, f32[8,64,128]{2,1,0:T(8,128)}) custom-call(bf16[8,8,64,128]{3,2,1,0:T(8,128)(2,1)} %misfit_in.1, f32[8,64,128]{2,1,0:T(8,128)} %bitcast.5, f32[8,64,128]{2,1,0:T(8,128)} %bitcast.6, f32[3,8,64,128]{3,2,1,0:T(8,128)} %coeffs_in.1), custom_call_target="tpu_custom_call" | custom-call | tf_op jit(solution)/shard_map/cycle/pallas_call | solution.py:547
  61.8 0.0 copy-done
  61.8 0.0 copy-start.1
  61.8 0.0 copy-start.2
  61.8 1.7 %add_bitcast_fusion = f32[1,8,64,128]{3,2,1,0:T(8,128)} fusion(f32[8,64,128]{2,1,0:T(8,128)} %get-tuple-element.4, f32[1,8,64,128]{3,2,1,0:T(8,128)S(1)} %copy-done), kind=kLoop, calls=%fused_computation.1 | loop fusion | flops 65536 | bytes 786432 | tf_op jit(solution)/shard_map/broadcast_in_dim | solution.py:565
  63.5 0.0 copy-done.1
  63.5 0.0 copy-done.2
  63.5 0.7 %multiply_add_fusion = f32[8,64,128]{2,1,0:T(8,128)} fusion(f32[8,64,128]{2,1,0:T(8,128)S(1)} %copy-done.2, f32[8,64,128]{2,1,0:T(8,128)S(1)} %copy-done.1), kind=kLoop, calls=%fused_computation | loop fusion | flops 196608 | bytes 786432 | tf_op jit(solution)/shard_map/add | solution.py:564
Async XLA Ops:
  0.6 61.1 %copy-start = (f32[1,8,64,128]{3,2,1,0:T(8,128)S(1)}, f32[1,8,64,128]{3,2,1,0:T(8,128)}, u32[]{:S(2)}) copy-start(f32[1,8,64,128]{3,2,1,0:T(8,128)} %param.6) | copy-start | bytes 786436
  61.8 1.8 %copy-start.1 = (f32[8,64,128]{2,1,0:T(8,128)S(1)}, f32[8,64,128]{2,1,0:T(8,128)}, u32[]{:S(2)}) copy-start(f32[8,64,128]{2,1,0:T(8,128)} %param.9) | copy-start | bytes 786436
  61.8 1.8 %copy-start.2 = (f32[8,64,128]{2,1,0:T(8,128)S(1)}, f32[8,64,128]{2,1,0:T(8,128)}, u32[]{:S(2)}) copy-start(f32[8,64,128]{2,1,0:T(8,128)} %get-tuple-element.5) | copy-start | bytes 786436

commit v2 on v1

--- a/solution.py
+++ b/solution.py
@@ -11,8 +11,7 @@
 NU = 0.14
 BETA = 0.5
 CENTRE = 1.0 - 6.0 * NU
-ROUNDS = (1, 1, 2, 2, 2)
-CUT = 99
+ROUNDS = (1, 2, 2, 3)
 MESH = pl.DeviceIdType.MESH
 F32 = jnp.float32
 MAX_MOVES = 64
@@ -74,7 +73,7 @@
             when(self.sent, lambda: self.copy(self.whole, self.whole, self.net.here).wait_send())
 
 
-def kernel(cfg, misfit_in, guess_in, rate_in, coeffs_in, e_out, total_out, *scratch):
+def kernel(cfg, misfit_in, guess_in, rate_in, coeffs_in, control_in, corrected_out, gradient_out, *scratch):
     buf = SimpleNamespace(**dict(zip(cfg.names, scratch)))
     wf = scratch[len(cfg.names):len(cfg.names) + len(cfg.rounds)]
     mids = scratch[len(cfg.names) + len(cfg.rounds):-4]
@@ -82,7 +81,7 @@
     guess, rate, coeffs = buf.guess, buf.rate, buf.coeffs
     fetches = [
         pltpu.make_async_copy(src, dst, inputs.at[i])
-        for i, (src, dst) in enumerate(((guess_in, guess), (coeffs_in, coeffs), (misfit_in, misfit), (rate_in, rate)))
+        for i, (src, dst) in enumerate(((guess_in, guess), (coeffs_in, coeffs), (misfit_in, misfit), (rate_in, rate), (control_in, buf.control)))
     ]
     for fetch in fetches:
         fetch.start()
@@ -115,15 +114,15 @@
         greet((base + (spot + i) % members, y))
         return 0
 
-    lax.fori_loop(1, members, greet_member, 0)
-    for i in range(1, groups):
-        greet(((x + i) % groups * members + spot, y))
     when(has_low, lambda: greet(below))
     when(has_high, lambda: greet(above))
     for exists, there in ((has_next, tm + 1), (has_before, tm - 1)):
         when(exists, lambda: greet((there, y)))
         when(exists & has_low, lambda: greet((there, y - 1)))
         when(exists & has_high, lambda: greet((there, y + 1)))
+    lax.fori_loop(1, members, greet_member, 0)
+    for i in range(1, groups):
+        greet(((x + i) % groups * members + spot, y))
     sides = has_low.astype(jnp.int32) + has_high.astype(jnp.int32)
     ends = has_next.astype(jnp.int32) + has_before.astype(jnp.int32)
 
@@ -137,8 +136,6 @@
                 buf.f_send[HIGH, k + i] = misfit[steps - 1 - turn, i].astype(F32)
 
     pl.semaphore_wait(barrier, members - 1 + groups - 1 + sides + ends + sides * ends)
-    if cfg.cut == 0:
-        return net.close()
 
     first = rounds[0]
     start = net.move(wf[0].at[pl.ds(first, rows)], has_before, has_next)
@@ -161,23 +158,32 @@
     def both_ends(src, at_low, at_high, dst):
         return up_down((src.at[at_high], dst.at[LOW]), (src.at[at_low], dst.at[HIGH]), dst.at[LOW], dst.at[HIGH])
 
-    def ends(src, width, dst, at=0):
-        low, high = pl.ds(at, width), pl.ds(rows - at - width, width)
-        to_low, to_high = pl.ds(deepest - at - width, width), pl.ds(at, width)
-        up, down = dst.at[LOW, to_low], dst.at[HIGH, to_high]
-        return up_down((src.at[high], up), (src.at[low], down), up, down)
-
-    beside = ends(coeffs.at[0], 1, buf.cx)
-    further = []
-    if deepest > 1:
-        count = deepest - 1
-        further.append(ends(coeffs.at[0], count, buf.cx, 1))
-        for i in range(2):
-            low, high = buf.cyz.at[LOW, i], buf.cyz.at[HIGH, i]
-            further.append(up_down(
-                (coeffs.at[1 + i, pl.ds(rows - count, count)], low), (coeffs.at[1 + i, pl.ds(0, count)], high), low, high))
-        low, high = buf.f_halo.at[LOW], buf.f_halo.at[HIGH]
-        further.append(up_down((buf.f_send.at[LOW], low), (buf.f_send.at[HIGH], high), low, high))
+    def ends(src, at, width, low_halo, high_halo, depth):
+        up, down = low_halo.at[pl.ds(depth - at - width, width)], high_halo.at[pl.ds(at, width)]
+        return up_down((src.at[pl.ds(rows - at - width, width)], up), (src.at[pl.ds(at, width)], down), up, down)
+
+    def reach_of(r):
+        before = max((0,) + rounds[:r])
+        after = max(before, rounds[r])
+        return before, after, max(before - 1, 0), after - 1
+
+    def near_stage(r):
+        before, after, yz_before, yz_after = reach_of(r)
+        moves = []
+        if after > before:
+            moves.append(ends(coeffs.at[0], before, after - before, buf.cx.at[LOW], buf.cx.at[HIGH], deepest))
+        if yz_after > yz_before:
+            for i in range(2):
+                moves.append(ends(coeffs.at[1 + i], yz_before, yz_after - yz_before, buf.cyz.at[LOW, i], buf.cyz.at[HIGH, i],
+                                  deepest - 1))
+        n = rounds[r]
+        if n > 1:
+            part = pl.ds(cfg.forcing_at[(r, 0)], n * (n - 1) // 2)
+            low, high = buf.f_halo.at[LOW, part], buf.f_halo.at[HIGH, part]
+            moves.append(up_down((buf.f_send.at[LOW, part], low), (buf.f_send.at[HIGH, part], high), low, high))
+        return moves
+
+    near = [near_stage(r) for r in range(min(2, len(rounds)))]
 
     def transpose(src, dst):
         move = net.move(dst.at[pl.ds(0, members - 1)])
@@ -228,13 +234,13 @@
             return 0
 
         if stop > start:
-            lax.fori_loop(start, stop, one, 0, unroll=unroll if (stop - start) % unroll == 0 else 1)
+            lax.fori_loop(start, stop, one, 0, unroll=min(unroll, stop - start))
 
     def own_factors(i):
         factors_x(wide + i, coeffs[0, i])
         factors_yz(wide + i, coeffs[1, i], coeffs[2, i])
 
-    each(0, rows, own_factors, 2)
+    each(0, rows, own_factors, 4)
 
     def clear(ref, start, count):
         def one(i):
@@ -242,8 +248,7 @@
 
         each(start, start + count, one)
 
-    halos = [(ref, n) for ref, n in zip(wf[1:], rounds[1:])] + [(ref, deepest - 1) for ref in mids]
-    halos += [(buf.e, wide), (buf.e1, wide), (buf.e2, wide)]
+    halos = [(ref, n) for ref, n in zip(wf[1:], rounds[1:])] + [(buf.e, wide), (buf.e1, wide), (buf.e2, wide)]
 
     @pl.when(jnp.logical_not(has_low))
     def _():
@@ -280,6 +285,8 @@
         else:
             forcing = buf.f_halo[HIGH, cfg.forcing_at[(r, s)] + row - rows]
         value = stepped(src, row + shift, row) + forcing
+        if side is not None:
+            value = jnp.where(has_low if side == LOW else has_high, value, 0.0)
         if s < n - 1:
             mids[s][row + deepest - 1] = value
         elif r < len(rounds) - 1:
@@ -294,31 +301,30 @@
 
     def inner(r):
         for s in range(rounds[r]):
-            each(s + 1, rows - 1 - s, lambda row: relax_row(r, s, row), 2)
-
-    def outer(r, side):
+            each(s + 1, rows - 1 - s, lambda row: relax_row(r, s, row), rows)
+
+    def outer(r):
         for s in range(rounds[r]):
             reach = rounds[r] - 1 - s
-            if side == LOW:
-                when(has_low, lambda: [relax_row(r, s, row, LOW) for row in range(-reach, 0)])
-                for row in range(s + 1):
-                    relax_row(r, s, row)
+            for i in range(reach):
+                relax_row(r, s, -1 - i, LOW)
+                relax_row(r, s, rows + i, HIGH)
+            for i in range(s + 1):
+                relax_row(r, s, i)
+                relax_row(r, s, rows - 1 - i)
+
+    def near_factors(r, side):
+        before, after, yz_before, yz_after = reach_of(r)
+        for k in range(before, after):
+            if side == HIGH:
+                factors_x(wide + rows + k, buf.cx[HIGH, k])
             else:
-                when(has_high, lambda: [relax_row(r, s, row, HIGH) for row in range(rows, rows + reach)])
-                for row in range(rows - 1 - s, rows):
-                    relax_row(r, s, row)
-
-    def beside_factors(side):
-        if side == HIGH:
-            factors_x(wide + rows, buf.cx[side, 0])
-        else:
-            factors_x(wide - 1, buf.cx[side, deepest - 1])
-
-    def further_factors(side):
-        at = wide + rows if side == HIGH else wide - deepest
-        each(0, deepest, lambda i: factors_x(at + i, buf.cx[side, i]))
-        at = wide + rows if side == HIGH else wide - deepest + 1
-        each(0, deepest - 1, lambda i: factors_yz(at + i, buf.cyz[side, 0, i], buf.cyz[side, 1, i]))
+                factors_x(wide - 1 - k, buf.cx[LOW, deepest - 1 - k])
+        for k in range(yz_before, yz_after):
+            if side == HIGH:
+                factors_yz(wide + rows + k, buf.cyz[HIGH, 0, k], buf.cyz[HIGH, 1, k])
+            else:
+                factors_yz(wide - 1 - k, buf.cyz[LOW, 0, deepest - 2 - k], buf.cyz[LOW, 1, deepest - 2 - k])
 
     def decays():
         rates.land()
@@ -336,38 +342,29 @@
             buf.upto[k] = upto
             return upto, summed + jnp.where((k > 0) | (x > 0), upto, 0.0)
 
-        buf.fx_send[0], buf.fx_send[1] = lax.fori_loop(1, members, one, (factor, factor))
+        buf.fx_send[0], buf.fx_send[1] = lax.fori_loop(1, members, one, (factor, factor), unroll=3)
         return across(buf.fx_send, buf.fx)
 
     start.land()
-    if cfg.cut == 20:
-        return net.close()
     faces = start_faces
     for r in range(len(rounds)):
         inner(r)
-        if r == len(rounds) - 2:
-            group_decay = decays()
         if r < len(rounds) - 1:
             n, ref = rounds[r + 1], wf[r + 1]
             low, high = ref.at[pl.ds(0, n)], ref.at[pl.ds(n + rows, n)]
             coming = net.move(low, has_high, has_low), net.move(high, has_low, has_high)
         for side, exists in ((LOW, has_low), (HIGH, has_high)):
-            if r == 0:
-                beside[side].land()
-                when(exists, lambda: beside_factors(side))
-            if rounds[r] > 1 and max((1,) + rounds[:r]) == 1:
-                for pair in further:
-                    pair[side].land()
-                when(exists, lambda: further_factors(side))
+            for pair in near[r]:
+                pair[side].land()
+            if near[r]:
+                when(exists, lambda: near_factors(r, side))
             faces[side].land()
-            outer(r, side)
-            if r < len(rounds) - 1:
-                if side == LOW:
-                    coming[HIGH].start(ref.at[pl.ds(n, n)], high, below)
-                else:
-                    coming[LOW].start(ref.at[pl.ds(rows, n)], low, above)
-        if cfg.cut == 1 + r:
-            return net.close()
+        outer(r)
+        if r < len(rounds) - 1:
+            coming[HIGH].start(ref.at[pl.ds(n, n)], high, below)
+            coming[LOW].start(ref.at[pl.ds(rows, n)], low, above)
+            if r + 2 < len(rounds):
+                near.append(near_stage(r + 2))
         if r == 0:
             rates = transpose(rate, buf.rates)
         if r < len(rounds) - 1:
@@ -381,9 +378,9 @@
         buf.far.at[LOW, :, :, mine], buf.far.at[HIGH, :, :, mine],
     )
 
+    group_decay = decays()
+
     terms.land()
-    if cfg.cut == 10:
-        return net.close()
     last = members - 1
     value = buf.terms[last]
     buf.local[last] = value
@@ -395,7 +392,7 @@
         buf.local[k] = value
         return value, summed + jnp.where((k > 0) | (x > 0), value, 0.0)
 
-    buf.rx_send[0], buf.rx_send[1] = lax.fori_loop(1, members, solve, (value, value))
+    buf.rx_send[0], buf.rx_send[1] = lax.fori_loop(1, members, solve, (value, value), unroll=5)
     group_result = across(buf.rx_send, buf.rx)
 
     pair.land()
@@ -403,7 +400,7 @@
     def pair_sum(i):
         buf.d_chip[i] = buf.d[i, mine] + buf.d_pair[i]
 
-    each(0, rows, pair_sum)
+    each(0, rows, pair_sum, rows)
     ring = along(lambda to: buf.d_chip.at[to], buf.d_ring.at[z], buf.d_ring.at[pl.ds(0, rows - 1)])
     buf.d_ring[z] = buf.d_chip[z]
 
@@ -415,8 +412,6 @@
 
     group_decay.land()
     group_result.land()
-    if cfg.cut == 11:
-        return net.close()
     carry = jnp.zeros((half, lanes), F32)
     e_sum = carry
     for group in reversed(range(groups)):
@@ -431,49 +426,23 @@
 
     carry = buf.carry[x]
 
-    def finish(k):
-        buf.back[k] = buf.local[k] + buf.upto[k] * carry
-
-    each(0, members, finish)
-    back = net.move(buf.back.at[pl.ds(0, members - 1)])
-
-    def send_back(i):
-        to = (spot + i) % members
-        back.start(buf.back.at[to], buf.e_own.at[z, mine], (base + to, y))
-
-    each(1, members, send_back)
-    buf.e_own[z, mine] = buf.back[spot]
+    def finish(i):
+        buf.back[i] = buf.local[2 * i + 1] + buf.upto[2 * i + 1] * carry
+
+    each(0, rows, finish, 4)
+    back = along(lambda to: buf.back.at[to], buf.e_own.at[z, mine], buf.e_own.at[pl.ds(0, rows - 1), mine])
+    buf.e_own[z, mine] = buf.back[z]
+
+    ring.land()
+    buf.dx_send[...] = lax.fori_loop(1, rows, lambda i, s: s + buf.d_ring[i], buf.d_ring[0])
+    d_across = across(buf.dx_send, buf.dx)
 
     e_ring.land()
-    if cfg.cut == 12:
-        return net.close()
     e_faces = up_down(
         (e.at[pl.ds(rows, wide), mine], e.at[rows_low, mine]), (e.at[pl.ds(wide, wide), mine], e.at[rows_high, mine]),
         e.at[rows_low, mine], e.at[rows_high, mine],
     )
     e_pair = net.move(e.at[rows_own, mine]).start(e.at[rows_own, mine], e.at[rows_own, mine], sibling)
-
-    ring.land()
-    buf.dx_send[...] = lax.fori_loop(1, rows, lambda i, s: s + buf.d_ring[i], buf.d_ring[0])
-    d_across = across(buf.dx_send, buf.dx)
-
-    def far_factors(side):
-        def one(i):
-            row = wide + rows + i if side == HIGH else i
-            factors_x(row, buf.far[side, 0, i])
-            factors_yz(row, buf.far[side, 1, i], buf.far[side, 2, i])
-
-        each(0, wide, one)
-
-    for side, exists in ((LOW, has_low), (HIGH, has_high)):
-        far_pair[side].land()
-        when(exists, lambda: far_factors(side))
-
-    e_pairs = [e_pair]
-    for side, exists, where in ((LOW, has_low, rows_low), (HIGH, has_high, rows_high)):
-        e_faces[side].land()
-        part = e.at[where, mine]
-        e_pairs.append(net.move(part, exists, exists).start(part, part, sibling))
 
     d_across.land()
     t_mine = buf.t_own[...]
@@ -482,39 +451,69 @@
     t[z, mine] = t_mine
     t_ring = along(lambda to: t.at[z, mine], t.at[z, mine], t.at[pl.ds(0, rows - 1), mine])
 
+    def far_factors(side):
+        def one(i):
+            row = wide + rows + i if side == HIGH else i
+            factors_x(row, buf.far[side, 0, i])
+            factors_yz(row, buf.far[side, 1, i], buf.far[side, 2, i])
+
+        each(0, wide, one, wide)
+
+    for side, exists in ((LOW, has_low), (HIGH, has_high)):
+        far_pair[side].land()
+        when(exists, lambda: far_factors(side))
+
+    e_pairs = [e_pair]
+    for side, exists, where in ((LOW, has_low, rows_low), (HIGH, has_high, rows_high)):
+        e_faces[side].land()
+        part = e.at[where, mine]
+        e_pairs.append(net.move(part, exists, exists).start(part, part, sibling))
+
     for pair in e_pairs:
         pair.land()
-    if cfg.cut == 13:
-        return net.close()
 
     for s in range(steps - 1):
-        if s == min(2, steps - 2):
+        if s == min(3, steps - 2):
             t_ring.land()
             t_pair = net.move(t.at[:, mine]).start(t.at[:, mine], t.at[:, mine], sibling)
+        if s == min(5, steps - 2):
+            back.land()
+            back_pair = net.move(buf.e_own.at[:, mine]).start(buf.e_own.at[:, mine], buf.e_own.at[:, mine], sibling)
         src = (e, buf.e1, buf.e2)[0 if s == 0 else 1 + (s - 1) % 2]
         dst = (buf.e1, buf.e2)[s % 2]
         reach = steps - 2 - s
 
-        def halo_row(row):
-            dst[row + wide] = stepped(src, row + wide, row)
+        def halo_row(row, exists):
+            dst[row + wide] = jnp.where(exists, stepped(src, row + wide, row), 0.0)
 
         def own_row(row):
             value = stepped(src, row + wide, row)
             dst[row + wide] = value
             buf.sum[row] = value if s == 0 else buf.sum[row] + value
 
-        when(has_low, lambda: each(-reach, 0, halo_row, 2))
-        when(has_high, lambda: each(rows, rows + reach, halo_row, 2))
-        each(0, rows, own_row, 2)
-
-    back.land()
-    e_out[...] = buf.e_own[...]
+        each(-reach, 0, lambda row: halo_row(row, has_low), rows)
+        each(0, rows, own_row, rows)
+        each(rows, rows + reach, lambda row: halo_row(row, has_high), rows)
+
     t_pair.land()
-    total_out[...] = t[...] + buf.sum[...]
+    buf.sum[...] = BETA * buf.control[...] + (t[...] + buf.sum[...]) * (1.0 / (slabs * steps))
+    results = [pltpu.make_async_copy(buf.sum, gradient_out, inputs.at[0])]
+    results[0].start()
+    back_pair.land()
+
+    def corrected_row(i):
+        later = buf.e_own[i]
+        buf.corrected[i] = guess[i] + jnp.where(core == 1, later, jnp.exp(-rate[i]) * later + buf.res[i])
+
+    each(0, rows, corrected_row, rows)
+    results.append(pltpu.make_async_copy(buf.corrected, corrected_out, inputs.at[1]))
+    results[1].start()
     net.close()
-
-
-def exchange(mesh, misfit, guess, rate, coeffs, rounds, cut):
+    for result in results:
+        result.wait()
+
+
+def exchange(mesh, misfit, guess, rate, coeffs, control, rounds):
     steps, rows, mid, lanes = misfit.shape
     members, half, wide = 2 * rows, mid // 2, steps - 1
     ny = mesh.shape[SPACE]
@@ -528,47 +527,45 @@
     plane, part = (mid, lanes), (half, lanes)
     field, long, slots = (rows,) + plane, (rows + 2 * wide,) + plane, (members,) + part
     shapes = dict(
-        guess=field, rate=field, coeffs=(3,) + field,
+        guess=field, rate=field, control=field, corrected=field, coeffs=(3,) + field,
         cx=(2, deepest) + plane, cyz=(2, 2, max(deepest - 1, 1)) + plane,
         f_send=(2, max(count, 1)) + plane, f_halo=(2, max(count, 1)) + plane,
         rates=slots, decay=slots, upto=slots, fx_send=(2,) + part, fx=(groups, 2) + part,
         res=field, d=field, d_pair=(rows,) + part, d_chip=(rows,) + part, d_ring=(rows,) + part,
         dx_send=part, dx=(groups,) + part, t_own=part,
         terms=slots, local=slots, rx_send=(2,) + part, rx=(groups, 2) + part,
-        carry=(groups,) + part, back=slots, e_own=field, t=field, sum=field, far=(2, 3, wide) + plane,
+        carry=(groups,) + part, back=(rows,) + part, e_own=field, t=field, sum=field, far=(2, 3, wide) + plane,
         ax=long, bx=long, ay=long, by=long, az=long, bz=long, e=long, e1=long, e2=long,
     )
     extra = [(rows + 2 * n,) + plane for n in rounds] + [(rows + 2 * (deepest - 1),) + plane] * (deepest - 1)
     cfg = SimpleNamespace(
         names=list(shapes), steps=steps, rounds=rounds, rows=rows, mid=mid, lanes=lanes, groups=groups, ny=ny,
-        forcing_at=forcing_at, cut=cut,
+        forcing_at=forcing_at,
     )
-    in_vmem, in_hbm = pl.BlockSpec(memory_space=pltpu.VMEM), pl.BlockSpec(memory_space=pltpu.HBM)
+    in_hbm = pl.BlockSpec(memory_space=pltpu.HBM)
     return pl.pallas_call(
         functools.partial(kernel, cfg),
         out_shape=[jax.ShapeDtypeStruct(field, F32)] * 2,
-        in_specs=[in_hbm] * 4,
-        out_specs=[in_vmem] * 2,
+        in_specs=[in_hbm] * 5,
+        out_specs=[in_hbm] * 2,
         scratch_shapes=[pltpu.VMEM(shape, F32) for shape in list(shapes.values()) + extra]
-        + [pltpu.VMEM(misfit.shape, misfit.dtype), pltpu.SemaphoreType.DMA((4,))]
+        + [pltpu.VMEM(misfit.shape, misfit.dtype), pltpu.SemaphoreType.DMA((5,))]
         + [pltpu.SemaphoreType.DMA((MAX_MOVES,))] * 2,
         compiler_params=pltpu.CompilerParams(
             collective_id=0, has_side_effects=True, vmem_limit_bytes=60 * 1024 * 1024),
         name="cycle",
-    )(misfit, guess, rate, coeffs)
-
-
-def on_device(mesh, rounds, cut, misfit, guess, rate, coeffs, control):
-    correction, total = exchange(mesh, misfit, guess[0], rate[0], coeffs, rounds, cut)
-    corrected = guess[0] + correction
-    gradient = BETA * control + total / (mesh.shape[TIME] * misfit.shape[0])
+    )(misfit, guess, rate, coeffs, control)
+
+
+def on_device(mesh, rounds, misfit, guess, rate, coeffs, control):
+    corrected, gradient = exchange(mesh, misfit, guess[0], rate[0], coeffs, control, rounds)
     return corrected[None], gradient
 
 
-def solution(mesh, rounds=ROUNDS, cut=CUT):
+def solution(mesh, rounds=ROUNDS):
     slab, block = P(TIME, SPACE, None, None), P(SPACE, None, None)
     return jax.shard_map(
-        functools.partial(on_device, mesh, rounds, cut),
+        functools.partial(on_device, mesh, rounds),
         mesh=mesh,
         in_specs=(slab, slab, slab, P(None, SPACE, None, None), block),
         out_specs=(slab, block),

time: 65.4 us -> 60.3 us (0.922); the launches traced: 64.3 us -> 60.2 us
  Pallas kernels: 61.1 us -> 57.1 us
  other arithmetic: 2.47 us -> 0 us
  local copies, waits for them, and re-layouts: 0.01 us -> 2.42 us
    pallas_call x1, Pallas kernels: 61.1 us -> 57.1 us  [exchange(): pl.pallas_call(functools.partial(kernel, cfg), out_shape=[jax.ShapeDtypeS...]
    unnamed x6 -> x4, local copies, waits for them, and re-layouts: 0.01 us -> 2.42 us
    broadcast_in_dim x1 -> x0, other arithmetic: 1.74 us -> none  [on_device(): return (corrected[None], gradient)]
    add x1 -> x0, other arithmetic: 0.74 us -> none  [on_device(): gradient = BETA * control + total / (mesh.shape[TIME] * misfit.shape[0])]
where the time goes in v2:
time: 60.3 us; the launch traced here: 60.2 us
  Pallas kernels  57.1 us (95%)
  local copies, waits for them, and re-layouts  2.42 us (4%)
  between operations  0.65 us (1%)
    pallas_call x1, Pallas kernels, exchange(): pl.pallas_call(functools.partial(kernel, cfg), out_shape=[jax.ShapeDtypeS...  57.1 us
    unnamed x4, local copies, waits for them, and re-layouts  2.42 us

profile of v2, /device:TPU:1, one launch (start us, length us, event | category | flops | bytes accessed | tf_op | source)
XLA Modules:
  0.0 60.2 jit_solution(10640488121306975155)
XLA Ops:
  0.6 57.1 %cycle.1 = (f32[8,64,128]{2,1,0:T(8,128)}, f32[8,64,128]{2,1,0:T(8,128)}) custom-call(bf16[8,8,64,128]{3,2,1,0:T(8,128)(2,1)} %misfit_in.1, f32[8,64,128]{2,1,0:T(8,128)} %bitcast.3, f32[8,64,128]{2,1,0:T(8,128)} %bitcast.4, f32[3,8,64,128]{3,2,1,0:T(8,128)} %coeffs_in.1, f32[8,64,128]{2,1,0:T(8,128)} %control_in.1), custom_call_target="tpu_custom_call" | custom-call | tf_op jit(solution)/shard_map/cycle/pallas_call | solution.py:546
  57.8 0.0 copy-start
  57.8 1.7 %copy.9 = f32[1,8,64,128]{3,2,1,0:T(8,128)} copy(f32[1,8,64,128]{3,2,1,0:T(8,128)} %bitcast.5) | data formatting | bytes 524288
  59.5 0.0 copy-done
  59.5 0.7 %copy.10 = f32[8,64,128]{2,1,0:T(8,128)} copy(f32[8,64,128]{2,1,0:T(8,128)S(1)} %copy-done) | data formatting | bytes 524288
Async XLA Ops:
  57.8 1.7 %copy-start = (f32[8,64,128]{2,1,0:T(8,128)S(1)}, f32[8,64,128]{2,1,0:T(8,128)}, u32[]{:S(2)}) copy-start(f32[8,64,128]{2,1,0:T(8,128)} %get-tuple-element.9) | copy-start | bytes 786436

commit v3 on v2

--- a/solution.py
+++ b/solution.py
@@ -31,6 +31,10 @@
         body()
     else:
         pl.when(condition)(body)
+
+
+def far_first(i, count):
+    return count // 2 + jnp.where(i % 2 == 0, i // 2, -(i // 2))
 
 
 class Net:
@@ -189,7 +193,7 @@
         move = net.move(dst.at[pl.ds(0, members - 1)])
 
         def send(i, _):
-            to = (spot + i) % members
+            to = (spot + far_first(i, members)) % members
             part = src.at[to // 2, pl.ds(pl.multiple_of(to % 2 * half, half), half)]
             move.start(part, dst.at[spot], (base + to, y))
             return 0
@@ -209,7 +213,7 @@
         move = net.move(whole)
 
         def send(i, _):
-            to = (z + i) % rows
+            to = (z + far_first(i, rows)) % rows
             move.start(source(to), target, (base + 2 * to + core, y))
             return 0
 
@@ -552,7 +556,7 @@
         + [pltpu.VMEM(misfit.shape, misfit.dtype), pltpu.SemaphoreType.DMA((5,))]
         + [pltpu.SemaphoreType.DMA((MAX_MOVES,))] * 2,
         compiler_params=pltpu.CompilerParams(
-            collective_id=0, has_side_effects=True, vmem_limit_bytes=60 * 1024 * 1024),
+            collective_id=0, has_side_effects=True, vmem_limit_bytes=213 * 256 * 1024),
         name="cycle",
     )(misfit, guess, rate, coeffs, control)
 

time: 60.3 us -> 57.6 us (0.955)
  Pallas kernels: 57.1 us -> 55.4 us
  local copies, waits for them, and re-layouts: 2.42 us -> 1.41 us
    pallas_call x1, Pallas kernels: 57.1 us -> 55.4 us  [exchange(): pl.pallas_call(functools.partial(kernel, cfg), out_shape=[jax.ShapeDtypeS...]
    unnamed x4 -> x2, local copies, waits for them, and re-layouts: 2.42 us -> 1.41 us
where the time goes in v3:
time: 57.6 us; the launch traced here: 57.4 us
  Pallas kernels  55.4 us (96%)
  local copies, waits for them, and re-layouts  1.41 us (2%)
  between operations  0.64 us (1%)
    pallas_call x1, Pallas kernels, exchange(): pl.pallas_call(functools.partial(kernel, cfg), out_shape=[jax.ShapeDtypeS...  55.4 us
    unnamed x2, local copies, waits for them, and re-layouts  1.41 us

profile of v3, /device:TPU:1, one launch (start us, length us, event | category | flops | bytes accessed | tf_op | source)
XLA Modules:
  0.0 57.4 jit_solution(837833280520327946)
XLA Ops:
  0.6 55.4 %cycle.1 = (f32[8,64,128]{2,1,0:T(8,128)S(1)}, f32[8,64,128]{2,1,0:T(8,128)S(1)}) custom-call(bf16[8,8,64,128]{3,2,1,0:T(8,128)(2,1)} %misfit_in.1, f32[8,64,128]{2,1,0:T(8,128)} %bitcast.4, f32[8,64,128]{2,1,0:T(8,128)} %bitcast.5, f32[3,8,64,128]{3,2,1,0:T(8,128)} %coeffs_in.1, f32[8,64,128]{2,1,0:T(8,128)} %control_in.1), custom_call_target="tpu_custom_call" | custom-call | tf_op jit(solution)/shard_map/cycle/pallas_call | solution.py:550
  56.0 0.7 %copy.9 = f32[1,8,64,128]{3,2,1,0:T(8,128)} copy(f32[1,8,64,128]{3,2,1,0:T(8,128)S(1)} %bitcast.3) | data formatting | bytes 524288
  56.7 0.7 %copy.10 = f32[8,64,128]{2,1,0:T(8,128)} copy(f32[8,64,128]{2,1,0:T(8,128)S(1)} %get-tuple-element.9) | data formatting | bytes 524288

commit v4 on v3

--- a/solution.py
+++ b/solution.py
@@ -115,18 +115,18 @@
         pl.semaphore_signal(barrier, inc=1, device_id=device, device_id_type=MESH)
 
     def greet_member(i, _):
-        greet((base + (spot + i) % members, y))
+        greet((base + (spot + far_first(i, members)) % members, y))
         return 0
 
+    lax.fori_loop(1, members, greet_member, 0, unroll=members - 1)
+    for i in range(1, groups):
+        greet(((x + i) % groups * members + spot, y))
     when(has_low, lambda: greet(below))
     when(has_high, lambda: greet(above))
     for exists, there in ((has_next, tm + 1), (has_before, tm - 1)):
         when(exists, lambda: greet((there, y)))
         when(exists & has_low, lambda: greet((there, y - 1)))
         when(exists & has_high, lambda: greet((there, y + 1)))
-    lax.fori_loop(1, members, greet_member, 0)
-    for i in range(1, groups):
-        greet(((x + i) % groups * members + spot, y))
     sides = has_low.astype(jnp.int32) + has_high.astype(jnp.int32)
     ends = has_next.astype(jnp.int32) + has_before.astype(jnp.int32)
 
@@ -204,7 +204,7 @@
 
     def across(src, dst):
         move = net.move(dst.at[pl.ds(0, groups - 1)])
-        for i in range(1, groups):
+        for i in sorted(range(1, groups), key=lambda i: -min(i, groups - i)):
             move.start(src, dst.at[x], ((x + i) % groups * members + spot, y))
         dst[x] = src[...]
         return move

time: 57.6 us -> 57 us (0.990)
  no operation moved by 1% of the time
where the time goes in v4:
time: 57 us; the launch traced here: 56.9 us
  Pallas kernels  54.9 us (96%)
  local copies, waits for them, and re-layouts  1.41 us (2%)
  between operations  0.64 us (1%)
    pallas_call x1, Pallas kernels, exchange(): pl.pallas_call(functools.partial(kernel, cfg), out_shape=[jax.ShapeDtypeS...  54.9 us
    unnamed x2, local copies, waits for them, and re-layouts  1.41 us

profile of v4, /device:TPU:1, one launch (start us, length us, event | category | flops | bytes accessed | tf_op | source)
XLA Modules:
  0.0 56.9 jit_solution(6943743667580799214)
XLA Ops:
  0.6 54.9 %cycle.1 = (f32[8,64,128]{2,1,0:T(8,128)S(1)}, f32[8,64,128]{2,1,0:T(8,128)S(1)}) custom-call(bf16[8,8,64,128]{3,2,1,0:T(8,128)(2,1)} %misfit_in.1, f32[8,64,128]{2,1,0:T(8,128)} %bitcast.4, f32[8,64,128]{2,1,0:T(8,128)} %bitcast.5, f32[3,8,64,128]{3,2,1,0:T(8,128)} %coeffs_in.1, f32[8,64,128]{2,1,0:T(8,128)} %control_in.1), custom_call_target="tpu_custom_call" | custom-call | tf_op jit(solution)/shard_map/cycle/pallas_call | solution.py:550
  55.5 0.7 %copy.9 = f32[1,8,64,128]{3,2,1,0:T(8,128)} copy(f32[1,8,64,128]{3,2,1,0:T(8,128)S(1)} %bitcast.3) | data formatting | bytes 524288
  56.2 0.7 %copy.10 = f32[8,64,128]{2,1,0:T(8,128)} copy(f32[8,64,128]{2,1,0:T(8,128)S(1)} %get-tuple-element.9) | data formatting | bytes 524288

commit v5 on v4

--- a/solution.py
+++ b/solution.py
@@ -198,7 +198,7 @@
             move.start(part, dst.at[spot], (base + to, y))
             return 0
 
-        lax.fori_loop(1, members, send, 0)
+        lax.fori_loop(1, members, send, 0, unroll=members - 1)
         dst[spot] = src[z, mine]
         return move
 
@@ -217,7 +217,7 @@
             move.start(source(to), target, (base + 2 * to + core, y))
             return 0
 
-        lax.fori_loop(1, rows, send, 0)
+        lax.fori_loop(1, rows, send, 0, unroll=rows - 1)
         return move
 
     def factors_x(row, c):
@@ -396,7 +396,7 @@
         buf.local[k] = value
         return value, summed + jnp.where((k > 0) | (x > 0), value, 0.0)
 
-    buf.rx_send[0], buf.rx_send[1] = lax.fori_loop(1, members, solve, (value, value), unroll=5)
+    buf.rx_send[0], buf.rx_send[1] = lax.fori_loop(1, members, solve, (value, value), unroll=members - 1)
     group_result = across(buf.rx_send, buf.rx)
 
     pair.land()

time: 57 us -> 57.1 us (level)
  no operation moved by 1% of the time
where the time goes in v5:
time: 57.1 us; the launch traced here: 56.9 us
  Pallas kernels  54.9 us (96%)
  local copies, waits for them, and re-layouts  1.41 us (2%)
  between operations  0.64 us (1%)
    pallas_call x1, Pallas kernels, exchange(): pl.pallas_call(functools.partial(kernel, cfg), out_shape=[jax.ShapeDtypeS...  54.9 us
    unnamed x2, local copies, waits for them, and re-layouts  1.41 us

profile of v5, /device:TPU:1, one launch (start us, length us, event | category | flops | bytes accessed | tf_op | source)
XLA Modules:
  0.0 56.9 jit_solution(925242665803896657)
XLA Ops:
  0.6 54.9 %cycle.1 = (f32[8,64,128]{2,1,0:T(8,128)S(1)}, f32[8,64,128]{2,1,0:T(8,128)S(1)}) custom-call(bf16[8,8,64,128]{3,2,1,0:T(8,128)(2,1)} %misfit_in.1, f32[8,64,128]{2,1,0:T(8,128)} %bitcast.4, f32[8,64,128]{2,1,0:T(8,128)} %bitcast.5, f32[3,8,64,128]{3,2,1,0:T(8,128)} %coeffs_in.1, f32[8,64,128]{2,1,0:T(8,128)} %control_in.1), custom_call_target="tpu_custom_call" | custom-call | tf_op jit(solution)/shard_map/cycle/pallas_call | solution.py:550
  55.5 0.7 %copy.9 = f32[1,8,64,128]{3,2,1,0:T(8,128)} copy(f32[1,8,64,128]{3,2,1,0:T(8,128)S(1)} %bitcast.3) | data formatting | bytes 524288
  56.2 0.7 %copy.10 = f32[8,64,128]{2,1,0:T(8,128)} copy(f32[8,64,128]{2,1,0:T(8,128)S(1)} %get-tuple-element.9) | data formatting | bytes 524288
